TPU v7x, 32 devices: a whole 2x2x4 slice. The times are simulated.
32 devices in a mesh: region: 4 (over y, x), blk: 8 (over z, core).
Axes of the slice: x: 2, y: 2, z: 4, core: 2. Of those that a mesh axis runs over, the one named last changes fastest.
Arguments:
- probes: bfloat16 [2, 16, 16384], P(None, None, ('region', 'blk')), may hold values from -6 to 6
- near_blocks: bfloat16 [3, 2, 16384, 512], P(None, None, ('region', 'blk')), may hold values from -0.078125 to 0.078125
- inner_basis: bfloat16 [2, 64, 16384], P(None, None, ('region', 'blk')), may hold values from -0.1875 to 0.1875
- coupling: bfloat16 [2, 2048, 512], P(None, ('region', 'blk')), may hold values from -0.1875 to 0.1875
- inner_expand: bfloat16 [2, 64, 16384], P(None, None, ('region', 'blk')), may hold values from -0.25 to 0.25
- outer_basis: bfloat16 [2, 256, 16384], P(None, None, ('region', 'blk')), may hold values from -0.1875 to 0.1875
- group_coupling: bfloat16 [2, 1024, 1024], P(None, 'region'), may hold values from -0.046875 to 0.046875
- outer_expand: bfloat16 [2, 256, 16384], P(None, None, ('region', 'blk')), may hold values from -0.125 to 0.125
- ranks: int32 [32], P(('region', 'blk')), may hold values from 8 to 64, as said below
Outputs:
- first: float32 [2, 16, 16384], P(None, None, ('region', 'blk'))
- second: float32 [2, 16, 16384], P(None, None, ('region', 'blk'))
Inputs may be any that keep to these rules, and one draw needn't show every extreme that they name: `ranks`: some cluster has rank 64.
All inputs are finite; a program needn't handle non-finite values.
Results may differ from a plain program's by a relative error of at most 0.004.
Values may be sent and summed in bfloat16 or wider, within the bound.
A program may use at most 64 MiB of HBM per device.

v0:
```python
import jax
import jax.numpy as jnp
from jax import lax
from jax.sharding import PartitionSpec as P


def padded_2(value, sides, width):
    for axis, dim in sides:
        devices, length = (lax.axis_size(axis), value.shape[dim])
        up = [(i, (i + 1) % devices) for i in range(devices - 1)]
        down = [(j, i) for i, j in up]
        last = lax.slice_in_dim(value, length - width, length, axis=dim)
        leading = lax.slice_in_dim(value, 0, width, axis=dim)
        before = lax.ppermute(last, axis, up)
        after = lax.ppermute(leading, axis, down)
        value = jnp.concatenate([before, value, after], axis=dim)
    return value


def dots(vec, mat):
    return jnp.dot(vec, mat.T, preferred_element_type=jnp.float32)


def cmul(mat, vec):
    real = dots(vec[0], mat[0]) - dots(vec[1], mat[1])
    imag = dots(vec[1], mat[0]) + dots(vec[0], mat[1])
    return jnp.stack([real, imag])


def cexpand(vec, mat):
    real = jnp.dot(vec[0], mat[0], preferred_element_type=jnp.float32) - jnp.dot(
        vec[1], mat[1], preferred_element_type=jnp.float32
    )
    imag = jnp.dot(vec[1], mat[0], preferred_element_type=jnp.float32) + jnp.dot(
        vec[0], mat[1], preferred_element_type=jnp.float32
    )
    return jnp.stack([real, imag])


def cmul_high(mat, vec):
    high = lax.Precision.HIGHEST
    real = jnp.dot(vec[0], mat[0].T, precision=high) - jnp.dot(vec[1], mat[1].T, precision=high)
    imag = jnp.dot(vec[1], mat[0].T, precision=high) + jnp.dot(vec[0], mat[1].T, precision=high)
    return jnp.stack([real, imag])


def apply_operator(
    vec,
    near_blocks,
    inner_basis,
    coupling,
    inner_expand,
    outer_basis,
    group_coupling,
    outer_expand,
    ranks,
):
    width = vec.shape[2]
    rank_cap = inner_basis.shape[1]
    group_rank = outer_basis.shape[1]
    position = lax.axis_index("blk")
    region_index = lax.axis_index("region")
    padded = padded_2(vec, (("blk", 2),), width)
    near = (
        cmul(near_blocks[0], padded[:, :, :width])
        + cmul(near_blocks[1], vec)
        + cmul(near_blocks[2], padded[:, :, 2 * width :])
    )
    keep = jnp.arange(rank_cap, dtype=jnp.int32) < ranks[0]
    coeff = cmul(inner_basis, vec)
    coeff = jnp.where(keep[None, None, :], coeff, jnp.zeros_like(coeff)).astype(jnp.bfloat16)
    piece = lax.all_gather(coeff, "blk", axis=2, tiled=True)
    columns = piece.shape[2]
    owners = jnp.arange(columns, dtype=jnp.int32) // rank_cap
    distant = jnp.abs(owners - position) > 1
    piece = jnp.where(distant[None, None, :], piece, jnp.zeros_like(piece))
    rows = coupling
    inner = cmul(rows, piece).astype(jnp.bfloat16)
    wide = cmul(outer_basis, vec)
    group_total = lax.psum(wide, "blk")
    piece = lax.all_gather(group_total, "region", axis=2, tiled=True)
    columns = piece.shape[2]
    owners = jnp.arange(columns, dtype=jnp.int32) // group_rank
    others = owners != region_index
    piece = jnp.where(others[None, None, :], piece, jnp.zeros_like(piece))
    rows = group_coupling.astype(jnp.float32)
    field = cmul_high(rows, piece)
    field = field.astype(jnp.bfloat16)
    return near + cexpand(inner, inner_expand) + cexpand(field, outer_expand)


def local(
    probes,
    near_blocks,
    inner_basis,
    coupling,
    inner_expand,
    outer_basis,
    group_coupling,
    outer_expand,
    ranks,
):
    first = apply_operator(
        probes,
        near_blocks,
        inner_basis,
        coupling,
        inner_expand,
        outer_basis,
        group_coupling,
        outer_expand,
        ranks,
    )
    second = apply_operator(
        first.astype(jnp.bfloat16),
        near_blocks,
        inner_basis,
        coupling,
        inner_expand,
        outer_basis,
        group_coupling,
        outer_expand,
        ranks,
    )
    return (first, second)


def solution(mesh):
    placed = (
        P(None, None, ("region", "blk")),
        P(None, None, ("region", "blk"), None),
        P(None, None, ("region", "blk")),
        P(None, ("region", "blk"), None),
        P(None, None, ("region", "blk")),
        P(None, None, ("region", "blk")),
        P(None, "region", None),
        P(None, None, ("region", "blk")),
        P(("region", "blk")),
    )
    return jax.shard_map(
        local,
        mesh=mesh,
        in_specs=placed,
        out_specs=(P(None, None, ("region", "blk")), P(None, None, ("region", "blk"))),
        check_vma=False,
    )
```

profile of v0, /device:TPU:1, one launch (start us, length us, event | category | flops | bytes accessed | tf_op | source)
XLA Modules:
  0.0 174.5 jit_solution(2569385095054770665)
XLA Ops:
  0.7 2.2 %collective-permute-start.1 = (bf16[2,16,512]{2,1,0:T(8,128)(2,1)}, bf16[2,16,512]{2,1,0:T(8,128)(2,1)S(1)}, u32[]{:S(2)}, u32[]{:S(2)}) collective-permute-start(bf16[2,16,512]{2,1,0:T(8,128)(2,1)} %param.9), channel_id=1, source_target_pairs={{1,0},{2,1},{3,2},{4,3},{5,4},{6,5},{7,6},{9,8},{10,9},{11,10},{12... | collective-permute-start | bytes 98312 | tf_op jit(solution)/shard_map/ppermute | solution.py:15
  2.9 4.6 %collective-permute-start = (bf16[2,16,512]{2,1,0:T(8,128)(2,1)}, bf16[2,16,512]{2,1,0:T(8,128)(2,1)S(1)}, u32[]{:S(2)}, u32[]{:S(2)}) collective-permute-start(bf16[2,16,512]{2,1,0:T(8,128)(2,1)} %param.9), channel_id=1, source_target_pairs={{0,1},{1,2},{2,3},{3,4},{4,5},{5,6},{6,7},{8,9},{9,10},{10,11},{11... | collective-permute-start | bytes 98312 | tf_op jit(solution)/shard_map/ppermute | solution.py:14
  12.3 14.8 %all_gather.12 = bf16[2,16,512]{1,0,2:T(2,128)(2,1)} all-gather(bf16[2,16,64]{1,0,2:T(2,128)(2,1)S(1)} %copy.13), channel_id=1, replica_groups=mesh['region'=4,'blk'=8] {'blk'}, dimensions={2}, use_global_device_ids=true | all-gather | bytes 36864 | tf_op jit(solution)/shard_map/all_gather | solution.py:72
  27.0 1.7 copy.14
  29.5 1.6 fusion.184
  31.0 1.6 fusion.182
  32.6 1.8 %fusion.136 = f32[16,256]{1,0:T(8,128)} fusion(bf16[2,256,512]{2,1,0:T(8,128)(2,1)} %param.14, bf16[2,16,512]{2,1,0:T(8,128)(2,1)} %param.9), kind=kOutput, calls=%fused_computation.172 | convolution fusion | flops 4194304 | bytes 294912 | tf_op jit(solution)/shard_map/dot_general | solution.py:21
  34.4 1.1 fusion.138
  36.1 1.1 fusion.22
  37.2 1.2 fusion.23
  39.0 26.4 %psum.14 = f32[2,16,256]{2,1,0:T(8,128)} all-reduce(f32[2,16,256]{2,1,0:T(8,128)} %pad_maximum_fusion), channel_id=1, replica_groups=mesh['region'=4,'blk'=8] {'blk'}, use_global_device_ids=true, to_apply=%region_0.1 | all-reduce | flops 8192 | bytes 65536 | tf_op jit(solution)/shard_map/psum | solution.py:80
  65.4 7.0 %all_gather.13 = f32[2,16,1024]{2,1,0:T(8,128)S(1)} all-gather(f32[2,16,256]{2,1,0:T(8,128)} %psum.14), channel_id=1, replica_groups=mesh['region'=4,'blk'=8] {'region'}, dimensions={2}, use_global_device_ids=true | all-gather | bytes 163840 | tf_op jit(solution)/shard_map/all_gather | solution.py:81
  73.1 1.6 fusion.46
  74.7 1.6 fusion.44
  89.5 28.8 %psum.15 = f32[2,16,256]{2,1,0:T(8,128)} all-reduce(f32[2,16,256]{2,1,0:T(8,128)} %pad_maximum_fusion.1), channel_id=1, replica_groups=mesh['region'=4,'blk'=8] {'blk'}, use_global_device_ids=true, to_apply=%region_1.2 | all-reduce | flops 8192 | bytes 65536 | tf_op jit(solution)/shard_map/psum | solution.py:80
  118.3 6.2 %all_gather.15 = f32[2,16,1024]{2,1,0:T(8,128)S(1)} all-gather(f32[2,16,256]{2,1,0:T(8,128)} %psum.15), channel_id=1, replica_groups=mesh['region'=4,'blk'=8] {'region'}, dimensions={2}, use_global_device_ids=true | all-gather | bytes 163840 | tf_op jit(solution)/shard_map/all_gather | solution.py:81
  124.6 2.2 %fusion.42 = f32[16,256]{1,0:T(8,128)} fusion(bf16[2,256,1024]{2,1,0:T(8,128)(2,1)} %param.15, f32[2,16,1024]{2,1,0:T(8,128)S(1)} %broadcast_select_fusion), kind=kOutput, calls=%fused_computation.78 | convolution fusion | flops 50331648 | bytes 606208 | tf_op jit(solution)/shard_map/dot_general | solution.py:42
  126.8 1.5 fusion.40
  132.5 21.3 %all_gather.14 = bf16[2,16,512]{1,0,2:T(2,128)(2,1)} all-gather(bf16[2,16,64]{1,0,2:T(2,128)(2,1)S(1)} %copy.15), channel_id=1, replica_groups=mesh['region'=4,'blk'=8] {'blk'}, dimensions={2}, use_global_device_ids=true | all-gather | bytes 36864 | tf_op jit(solution)/shard_map/all_gather | solution.py:72
  155.9 2.1 %collective-permute-start.3 = (bf16[2,16,512]{2,1,0:T(8,128)(2,1)}, bf16[2,16,512]{2,1,0:T(8,128)(2,1)S(1)}, u32[]{:S(2)}, u32[]{:S(2)}) collective-permute-start(bf16[2,16,512]{2,1,0:T(8,128)(2,1)} %copy-done.8), channel_id=1, source_target_pairs={{1,0},{2,1},{3,2},{4,3},{5,4},{6,5},{7,6},{9,8},{10,9},{11,10},{12... | collective-permute-start | bytes 98312 | tf_op jit(solution)/shard_map/ppermute | solution.py:15
  159.9 3.5 %collective-permute-start.2 = (bf16[2,16,512]{2,1,0:T(8,128)(2,1)}, bf16[2,16,512]{2,1,0:T(8,128)(2,1)S(1)}, u32[]{:S(2)}, u32[]{:S(2)}) collective-permute-start(bf16[2,16,512]{2,1,0:T(8,128)(2,1)} %copy-done.8), channel_id=1, source_target_pairs={{0,1},{1,2},{2,3},{3,4},{4,5},{5,6},{6,7},{8,9},{9,10},{10,11},{11... | collective-permute-start | bytes 98312 | tf_op jit(solution)/shard_map/ppermute | solution.py:14
  163.4 1.6 fusion.26
  165.0 1.1 fusion.122
  166.0 1.6 fusion.27
  (111 shorter events, 35.0 us)
Async XLA Ops:
  0.6 75.6 %copy-start.10 = (bf16[2,16,512]{2,1,0:T(8,128)(2,1)S(1)}, bf16[2,16,512]{2,1,0:T(8,128)(2,1)}, u32[]{:S(2)}) copy-start(bf16[2,16,512]{2,1,0:T(8,128)(2,1)} %param.9) | copy-start | bytes 98308
  0.6 76.1 %copy-start.6 = (bf16[2,64,512]{2,1,0:T(8,128)(2,1)S(1)}, bf16[2,64,512]{2,1,0:T(8,128)(2,1)}, u32[]{:S(2)}) copy-start(bf16[2,64,512]{2,1,0:T(8,128)(2,1)} %param.12) | copy-start | bytes 393220
  0.7 75.6 %copy-start = (bf16[3,2,512,512]{3,2,1,0:T(8,128)(2,1)S(1)}, bf16[3,2,512,512]{3,2,1,0:T(8,128)(2,1)}, u32[]{:S(2)}) copy-start(bf16[3,2,512,512]{3,2,1,0:T(8,128)(2,1)} %param.10) | copy-start | bytes 9437188
  0.7 77.8 %copy-start.7 = (bf16[2,64,512]{2,1,0:T(8,128)(2,1)S(1)}, bf16[2,64,512]{2,1,0:T(8,128)(2,1)}, u32[]{:S(2)}) copy-start(bf16[2,64,512]{2,1,0:T(8,128)(2,1)} %param.13) | copy-start | bytes 393220
  0.7 80.5 %collective-permute-start.1 = (bf16[2,16,512]{2,1,0:T(8,128)(2,1)}, bf16[2,16,512]{2,1,0:T(8,128)(2,1)S(1)}, u32[]{:S(2)}, u32[]{:S(2)}) collective-permute-start(bf16[2,16,512]{2,1,0:T(8,128)(2,1)} %param.9), channel_id=1, source_target_pairs={{1,0},{2,1},{3,2},{4,3},{5,4},{6,5},{7,6},{9,8},{10,9},{11,10},{12... | collective-permute-start | bytes 98312 | tf_op jit(solution)/shard_map/ppermute | solution.py:15
  2.9 78.7 %collective-permute-start = (bf16[2,16,512]{2,1,0:T(8,128)(2,1)}, bf16[2,16,512]{2,1,0:T(8,128)(2,1)S(1)}, u32[]{:S(2)}, u32[]{:S(2)}) collective-permute-start(bf16[2,16,512]{2,1,0:T(8,128)(2,1)} %param.9), channel_id=1, source_target_pairs={{0,1},{1,2},{2,3},{3,4},{4,5},{5,6},{6,7},{8,9},{9,10},{10,11},{11... | collective-permute-start | bytes 98312 | tf_op jit(solution)/shard_map/ppermute | solution.py:14
  9.5 23.1 %copy-start.14 = (pred[512]{0:T(512)(128)(4,1)}, pred[512]{0:T(512)(128)(4,1)S(1)}, u32[]{:S(2)}) copy-start(pred[512]{0:T(512)(128)(4,1)S(1)} %fusion.254) | copy-start | bytes 1540
  10.1 2.0 %copy-start.15 = (pred[64]{0:T(512)(128)(4,1)}, pred[64]{0:T(512)(128)(4,1)S(1)}, u32[]{:S(2)}) copy-start(pred[64]{0:T(512)(128)(4,1)S(1)} %iota_compare_fusion) | copy-start | bytes 196
  65.4 13.4 %copy-start.1 = (bf16[2,256,1024]{2,1,0:T(8,128)(2,1)S(1)}, bf16[2,256,1024]{2,1,0:T(8,128)(2,1)}, u32[]{:S(2)}) copy-start(bf16[2,256,1024]{2,1,0:T(8,128)(2,1)} %param.15) | copy-start | bytes 3145732
  65.4 14.5 %copy-start.3 = (bf16[2,256,512]{2,1,0:T(8,128)(2,1)S(1)}, bf16[2,256,512]{2,1,0:T(8,128)(2,1)}, u32[]{:S(2)}) copy-start(bf16[2,256,512]{2,1,0:T(8,128)(2,1)} %param.16) | copy-start | bytes 1572868
  80.5 7.7 %copy-start.2 = (bf16[2,256,512]{2,1,0:T(8,128)(2,1)S(1)}, bf16[2,256,512]{2,1,0:T(8,128)(2,1)}, u32[]{:S(2)}) copy-start(bf16[2,256,512]{2,1,0:T(8,128)(2,1)} %param.14) | copy-start | bytes 1572868
  81.1 0.6 copy-start.12
  81.4 43.2 %copy-start.13 = (pred[1024]{0:T(1024)(128)(4,1)S(1)}, pred[1024]{0:T(1024)(128)(4,1)}, u32[]{:S(2)}) copy-start(pred[1024]{0:T(1024)(128)(4,1)} %fusion.248) | copy-start | bytes 3076
  81.8 0.6 copy-start.11
  82.6 45.8 %copy-start.5 = (bf16[2,64,512]{2,1,0:T(8,128)(2,1)S(1)}, bf16[2,64,512]{2,1,0:T(8,128)(2,1)}, u32[]{:S(2)}) copy-start(bf16[2,64,512]{2,1,0:T(8,128)(2,1)} %param.11) | copy-start | bytes 393220
  88.2 0.7 copy-start.8
  124.6 7.2 %copy-start.9 = (f32[2,16,1024]{2,1,0:T(8,128)}, f32[2,16,1024]{2,1,0:T(8,128)S(1)}, u32[]{:S(2)}) copy-start(f32[2,16,1024]{2,1,0:T(8,128)S(1)} %broadcast_select_fusion) | copy-start | bytes 393220
  154.9 13.9 %copy-start.4 = (bf16[2,256,512]{2,1,0:T(8,128)(2,1)S(1)}, bf16[2,256,512]{2,1,0:T(8,128)(2,1)}, u32[]{:S(2)}) copy-start(bf16[2,256,512]{2,1,0:T(8,128)(2,1)} %param.16) | copy-start | bytes 1572868
  155.9 15.9 %collective-permute-start.3 = (bf16[2,16,512]{2,1,0:T(8,128)(2,1)}, bf16[2,16,512]{2,1,0:T(8,128)(2,1)S(1)}, u32[]{:S(2)}, u32[]{:S(2)}) collective-permute-start(bf16[2,16,512]{2,1,0:T(8,128)(2,1)} %copy-done.8), channel_id=1, source_target_pairs={{1,0},{2,1},{3,2},{4,3},{5,4},{6,5},{7,6},{9,8},{10,9},{11,10},{12... | collective-permute-start | bytes 98312 | tf_op jit(solution)/shard_map/ppermute | solution.py:15
  159.9 12.4 %collective-permute-start.2 = (bf16[2,16,512]{2,1,0:T(8,128)(2,1)}, bf16[2,16,512]{2,1,0:T(8,128)(2,1)S(1)}, u32[]{:S(2)}, u32[]{:S(2)}) collective-permute-start(bf16[2,16,512]{2,1,0:T(8,128)(2,1)} %copy-done.8), channel_id=1, source_target_pairs={{0,1},{1,2},{2,3},{3,4},{4,5},{5,6},{6,7},{8,9},{9,10},{10,11},{11... | collective-permute-start | bytes 98312 | tf_op jit(solution)/shard_map/ppermute | solution.py:14
where the time goes:
time: 177 us; the launch traced here: 174 us
  blocking collectives  104 us (59%)
  matrix products  46.2 us (26%)
  starting transfers between devices  12.4 us (7%)
  other arithmetic  6.1 us (3%)
  local copies, waits for them, and re-layouts  3.83 us (2%)
    psum x2, blocking collectives, apply_operator(): group_total = lax.psum(wide, 'blk')  55.2 us
    all_gather x2, blocking collectives, apply_operator(): piece = lax.all_gather(coeff, 'blk', axis=2, tiled=True)  36 us
    dot_general x48, matrix products, dots(): return jnp.dot(vec, mat.T, preferred_element_type=jnp.float32)  31 us
    all_gather x2, blocking collectives, apply_operator(): piece = lax.all_gather(group_total, 'region', axis=2, tiled=True)  13.3 us
    ppermute x2, starting transfers between devices, padded_2(): before = lax.ppermute(last, axis, up)  8.06 us
    ppermute x2, starting transfers between devices, padded_2(): after = lax.ppermute(leading, axis, down)  4.31 us
    dot_general x2, matrix products, cmul_high(): jnp.dot(vec[0], mat[0].T, precision=high)  3.77 us
  transfers between devices with their start and end apart: 4, of which 0 were waited for; matrix products, arithmetic and copies ran while one was open for 21% of the time, Pallas kernels for 0%

commit v1 on v0

v1 whole, which is shorter than its diff:
```python
import functools

import jax
import jax.numpy as jnp
from jax import lax
from jax.experimental import pallas as pl
from jax.experimental.pallas import tpu as pltpu
from jax.sharding import PartitionSpec as P

MESH = pl.DeviceIdType.MESH
F32 = jnp.float32
BF16 = jnp.bfloat16
TILE = 8
HALF = TILE // 2


def dot_t(vec, mat):
    return lax.dot_general(vec, mat, (((1,), (1,)), ((), ())), preferred_element_type=F32)


def dot(vec, mat):
    return jnp.dot(vec, mat, preferred_element_type=F32)


def times_i(x):
    rows, cols = x.shape
    x = x.reshape(rows // TILE, TILE, cols)
    turned = pltpu.roll(x, HALF, 1)
    upper = lax.broadcasted_iota(jnp.int32, x.shape, 1) < HALF
    return jnp.where(upper, -turned, turned).reshape(rows, cols)


def kernel(
    n_reg,
    n_blk,
    probes,
    near_blocks,
    inner_basis,
    coupling,
    inner_expand,
    outer_basis,
    group_coupling,
    outer_expand,
    ranks,
    first,
    second,
    v_in,
    nb,
    ib,
    cp,
    ie,
    ob,
    gc,
    oe,
    vbuf,
    nbr,
    wide_send,
    wide_recv,
    cbuf,
    fbuf,
    kmat,
    acc,
    load_sem,
    nbr_send,
    nbr_recv,
    wide_ssem,
    wide_rsem,
    c_ssem,
    c_rsem,
    f_ssem,
    f_rsem,
):
    region = lax.axis_index("region")
    pos = lax.axis_index("blk")
    rank_cap = ib.shape[1]
    group_rank = ob.shape[1]
    pages = wide_send.shape[1]
    stride = n_blk // pages
    slot = pos // stride
    reducer = lax.rem(pos, stride) == 0

    loads = [
        pltpu.make_async_copy(probes, v_in, load_sem.at[0]),
        pltpu.make_async_copy(outer_basis, ob, load_sem.at[1]),
        pltpu.make_async_copy(inner_basis, ib, load_sem.at[2]),
        pltpu.make_async_copy(near_blocks.at[1], nb.at[1], load_sem.at[3]),
        pltpu.make_async_copy(coupling, cp, load_sem.at[4]),
        pltpu.make_async_copy(group_coupling, gc, load_sem.at[5]),
        pltpu.make_async_copy(near_blocks.at[0], nb.at[0], load_sem.at[6]),
        pltpu.make_async_copy(near_blocks.at[2], nb.at[2], load_sem.at[7]),
        pltpu.make_async_copy(inner_expand, ie, load_sem.at[8]),
        pltpu.make_async_copy(outer_expand, oe, load_sem.at[9]),
    ]
    for load in loads:
        load.start()

    barrier = pltpu.get_barrier_semaphore()
    for off in range(1, n_blk):
        pl.semaphore_signal(
            barrier, inc=1, device_id=(region, lax.rem(pos + off, n_blk)), device_id_type=MESH
        )

    @pl.when(reducer)
    def _():
        for off in range(1, n_reg):
            for j in range(n_blk):
                pl.semaphore_signal(
                    barrier, inc=1, device_id=(lax.rem(region + off, n_reg), j), device_id_type=MESH
                )

    loads[0].wait()
    parts = [v_in[0].astype(F32), v_in[1].astype(F32)]
    start = jnp.concatenate(
        [parts[c][k * HALF : (k + 1) * HALF] for k in range(pages) for c in range(2)], axis=0
    )
    pl.semaphore_wait(barrier, n_blk - 1 + (n_reg - 1) * pages)

    def to_next(a):
        return pltpu.make_async_remote_copy(
            src_ref=vbuf.at[a],
            dst_ref=nbr.at[a, 0],
            send_sem=nbr_send.at[a, 0],
            recv_sem=nbr_recv.at[a, 0],
            device_id=(region, pos + 1),
            device_id_type=MESH,
        )

    def to_prev(a):
        return pltpu.make_async_remote_copy(
            src_ref=vbuf.at[a],
            dst_ref=nbr.at[a, 1],
            send_sem=nbr_send.at[a, 1],
            recv_sem=nbr_recv.at[a, 1],
            device_id=(region, pos - 1),
            device_id_type=MESH,
        )

    def wait_bytes(ref, sem):
        pltpu.make_async_copy(ref, ref, sem).wait()

    def apply(a, full):
        vec, ivec = full.astype(BF16), times_i(full).astype(BF16)
        vbuf[a] = vec

        @pl.when(pos < n_blk - 1)
        def _():
            to_next(a).start()

        @pl.when(pos > 0)
        def _():
            to_prev(a).start()

        if a == 0:
            loads[1].wait()
        wide = dot_t(vec, ob[0]) + dot_t(ivec, ob[1])
        wide_send[a] = wide.reshape(pages, TILE, group_rank)
        for off in range(1, n_reg):
            for k in range(pages):
                pltpu.make_async_remote_copy(
                    src_ref=wide_send.at[a, k],
                    dst_ref=wide_recv.at[a, off - 1, pos],
                    send_sem=wide_ssem.at[a],
                    recv_sem=wide_rsem.at[a],
                    device_id=(lax.rem(region + off, n_reg), k * stride),
                    device_id_type=MESH,
                ).start()

        if a == 0:
            loads[2].wait()
        coeff = dot_t(vec, ib[0]) + dot_t(ivec, ib[1])
        keep = lax.broadcasted_iota(jnp.int32, coeff.shape, 1) < ranks[0]
        coeff = jnp.where(keep, coeff, 0.0)
        cbuf[a, pos] = jnp.concatenate([coeff, times_i(coeff)], axis=1).astype(BF16)
        for off in range(1, n_blk):
            pltpu.make_async_remote_copy(
                src_ref=cbuf.at[a, pos],
                dst_ref=cbuf.at[a, pos],
                send_sem=c_ssem.at[a],
                recv_sem=c_rsem.at[a],
                device_id=(region, lax.rem(pos + off, n_blk)),
                device_id_type=MESH,
            ).start()

        if a == 0:
            loads[3].wait()
        acc[...] = dot_t(vec, nb[1, 0]) + dot_t(ivec, nb[1, 1])

        if a == 0:
            loads[4].wait()
            width = 2 * rank_cap
            lower = lax.broadcasted_iota(jnp.int32, (rank_cap, width), 1) < rank_cap
            for t in range(n_blk // 2):
                re = cp[0, :, t * width : (t + 1) * width].astype(F32)
                im = cp[1, :, t * width : (t + 1) * width].astype(F32)
                even = jnp.where(lower, re, pltpu.roll(im, rank_cap, 1))
                odd = jnp.where(lower, pltpu.roll(re, rank_cap, 1), im)
                for j, block in ((2 * t, even), (2 * t + 1, odd)):
                    far = (jnp.abs(pos - j) > 1).astype(F32)
                    kmat[:, j * width : (j + 1) * width] = (block * far).astype(BF16)
            loads[5].wait()

        @pl.when(reducer)
        def _():
            wait_bytes(wide_recv.at[a], wide_rsem.at[a])
            field = jnp.zeros((2 * TILE, group_rank), F32)
            for off in range(1, n_reg):
                total = wide_recv[a, off - 1, 0]
                for j in range(1, n_blk):
                    total = total + wide_recv[a, off - 1, j]
                high = total.astype(BF16).astype(F32)
                both = jnp.concatenate([high, total - high], axis=0)
                source = lax.rem(region - off + n_reg, n_reg)
                columns = pl.ds(pl.multiple_of(source * group_rank, group_rank), group_rank)
                field = field + dot_t(both.astype(BF16), gc[0, :, columns])
                field = field + dot_t(times_i(both).astype(BF16), gc[1, :, columns])
            fbuf[a, slot] = (field[:TILE] + field[TILE:]).astype(BF16).astype(F32)
            for off in range(1, n_blk):
                pltpu.make_async_remote_copy(
                    src_ref=fbuf.at[a, slot],
                    dst_ref=fbuf.at[a, slot],
                    send_sem=f_ssem.at[a],
                    recv_sem=f_rsem.at[a],
                    device_id=(region, lax.rem(pos + off, n_blk)),
                    device_id_type=MESH,
                ).start()

        if a == 0:
            loads[6].wait()
            loads[7].wait()

        @pl.when(pos > 0)
        def _():
            wait_bytes(nbr.at[a, 0], nbr_recv.at[a, 0])
            before = nbr[a, 0]
            turned = times_i(before.astype(F32)).astype(BF16)
            acc[...] += dot_t(before, nb[0, 0]) + dot_t(turned, nb[0, 1])

        @pl.when(pos < n_blk - 1)
        def _():
            wait_bytes(nbr.at[a, 1], nbr_recv.at[a, 1])
            after = nbr[a, 1]
            turned = times_i(after.astype(F32)).astype(BF16)
            acc[...] += dot_t(after, nb[2, 0]) + dot_t(turned, nb[2, 1])

        wait_bytes(cbuf.at[a, pl.ds(0, n_blk - 1)], c_rsem.at[a])
        piece = jnp.concatenate([cbuf[a, j] for j in range(n_blk)], axis=1)
        inner = dot_t(piece, kmat[...])
        if a == 0:
            loads[8].wait()
        acc[...] += dot(inner.astype(BF16), ie[0]) + dot(times_i(inner).astype(BF16), ie[1])

        if a == 0:
            loads[9].wait()

        @pl.when(reducer)
        def _():
            wait_bytes(fbuf.at[a, pl.ds(0, pages - 1)], f_rsem.at[a])

        @pl.when(jnp.logical_not(reducer))
        def _():
            wait_bytes(fbuf.at[a], f_rsem.at[a])

        field = fbuf[a].reshape(pages * TILE, group_rank)
        return acc[...] + dot(field.astype(BF16), oe[0]) + dot(times_i(field).astype(BF16), oe[1])

    def put(out, full):
        for k in range(pages):
            for c in range(2):
                lo = k * TILE + c * HALF
                out[c, k * HALF : (k + 1) * HALF, :] = full[lo : lo + HALF]

    one = apply(0, start)
    put(first, one)
    two = apply(1, one)
    put(second, two)

    for a in range(2):

        @pl.when(pos < n_blk - 1)
        def _():
            to_next(a).wait_send()

        @pl.when(pos > 0)
        def _():
            to_prev(a).wait_send()

        wait_bytes(wide_recv.at[a, :, pl.ds(0, pages)], wide_ssem.at[a])
        wait_bytes(cbuf.at[a, pl.ds(0, n_blk - 1)], c_ssem.at[a])

        @pl.when(reducer)
        def _():
            wait_bytes(wide_recv.at[a, 0, pl.ds(0, n_blk - 1)], f_ssem.at[a])


def solution(mesh):
    n_reg, n_blk = mesh.shape["region"], mesh.shape["blk"]
    both = ("region", "blk")

    def local(*args):
        probes, near_blocks, inner_basis, coupling, inner_expand = args[:5]
        outer_basis, group_coupling, outer_expand, _ = args[5:]
        _, vectors, width = probes.shape
        rows = 2 * vectors
        pages = rows // TILE
        rank_cap, group_rank = inner_basis.shape[1], outer_basis.shape[1]
        out = jax.ShapeDtypeStruct(probes.shape, F32)
        dma = pltpu.SemaphoreType.DMA
        return pl.pallas_call(
            functools.partial(kernel, n_reg, n_blk),
            out_shape=(out, out),
            in_specs=[pl.BlockSpec(memory_space=pl.ANY)] * 8
            + [pl.BlockSpec(memory_space=pltpu.SMEM)],
            out_specs=(pl.BlockSpec(memory_space=pltpu.VMEM),) * 2,
            scratch_shapes=[
                pltpu.VMEM(x.shape, BF16)
                for x in (
                    probes,
                    near_blocks,
                    inner_basis,
                    coupling,
                    inner_expand,
                    outer_basis,
                    group_coupling,
                    outer_expand,
                )
            ]
            + [
                pltpu.VMEM((2, rows, width), BF16),
                pltpu.VMEM((2, 2, rows, width), BF16),
                pltpu.VMEM((2, pages, TILE, group_rank), F32),
                pltpu.VMEM((2, n_reg - 1, n_blk, TILE, group_rank), F32),
                pltpu.VMEM((2, n_blk, rows, 2 * rank_cap), BF16),
                pltpu.VMEM((2, pages, TILE, group_rank), F32),
                pltpu.VMEM((rank_cap, n_blk * 2 * rank_cap), BF16),
                pltpu.VMEM((rows, width), F32),
                dma((10,)),
                dma((2, 2)),
                dma((2, 2)),
                dma((2,)),
                dma((2,)),
                dma((2,)),
                dma((2,)),
                dma((2,)),
                dma((2,)),
            ],
            compiler_params=pltpu.CompilerParams(
                collective_id=0, has_side_effects=True, vmem_limit_bytes=56 * 2**20
            ),
        )(*args)

    placed = (
        P(None, None, both),
        P(None, None, both, None),
        P(None, None, both),
        P(None, both, None),
        P(None, None, both),
        P(None, None, both),
        P(None, "region", None),
        P(None, None, both),
        P(both),
    )
    return jax.shard_map(
        local,
        mesh=mesh,
        in_specs=placed,
        out_specs=(P(None, None, both), P(None, None, both)),
        check_vma=False,
    )
```

time: 177 us -> 32.4 us (0.18); the launches traced: 174 us -> 31.8 us
  blocking collectives: 104 us -> 0 us
  matrix products: 46.2 us -> 0 us
  Pallas kernels: 0 us -> 27.6 us
  starting transfers between devices: 12.4 us -> 0 us
  other arithmetic: 6.1 us -> 0 us
    psum x2 -> x0, blocking collectives: 55.2 us -> none  [apply_operator(): group_total = lax.psum(wide, 'blk')]
    all_gather x4 -> x0, blocking collectives: 49.3 us -> none  [the longest x2 36 us: apply_operator(): piece = lax.all_gather(coeff, 'blk', axis=2, tiled=True)]
    dot_general x72 -> x0, matrix products: 46.2 us -> none  [the longest x48 31 us: dots(): return jnp.dot(vec, mat.T, preferred_element_type=jnp.float32)]
    pallas_call x0 -> x1, Pallas kernels: none -> 27.6 us  [local(): pl.pallas_call(functools.partial(kernel, n_reg, n_blk), out_shape=(out, o...]
    ppermute x4 -> x0, starting transfers between devices: 12.4 us -> none  [the longest x2 8.06 us: padded_2(): before = lax.ppermute(last, axis, up)]
    all_gather x2 -> x0, local copies, waits for them, and re-layouts: 2.77 us -> none  [apply_operator(): piece = lax.all_gather(coeff, 'blk', axis=2, tiled=True)]
    select_n x4 -> x0, other arithmetic: 2.19 us -> none  [the longest x2 1.5 us: apply_operator(): piece = jnp.where(distant[None, None, :], piece, jnp.zeros_like(piece))]
    unnamed x32 -> x2, local copies, waits for them, and re-layouts: 0.85 us -> 2.95 us
  transfers between devices with their start and end apart: 4 -> 0, of which waited for: 0 -> 0; matrix products, arithmetic and copies ran while one was open for 21% -> 0% of each run, Pallas kernels for 0% -> 0%
where the time goes in v1:
time: 32.4 us; the launch traced here: 31.8 us
  Pallas kernels  27.6 us (85%)
  local copies, waits for them, and re-layouts  2.95 us (9%)
  between operations  1.29 us (4%)
    pallas_call x1, Pallas kernels, local(): pl.pallas_call(functools.partial(kernel, n_reg, n_blk), out_shape=(out, o...  27.6 us
    unnamed x2, local copies, waits for them, and re-layouts  2.95 us

profile of v1, /device:TPU:1, one launch (start us, length us, event | category | flops | bytes accessed | tf_op | source)
XLA Modules:
  0.0 31.8 jit_solution(4732735529697345423)
XLA Ops:
  1.3 27.6 %shard_map.104 = (f32[2,16,512]{2,1,0:T(8,128)}, f32[2,16,512]{2,1,0:T(8,128)}) custom-call(bf16[2,16,512]{2,1,0:T(8,128)(2,1)} %probes.1, bf16[3,2,512,512]{3,2,1,0:T(8,128)(2,1)} %near_blocks.1, bf16[2,64,512]{2,1,0:T(8,128)(2,1)} %inner_basis.1, bf16[2,64,512]{2,1,0:T(8,128)(2,1)} %coupling.1, bf16[2,64,512]{2,1,0:T(8,128)(2,1)} %inner_expand.1, ...), custom_call_target="tpu_custom_call" | custom-call | tf_op jit(solution)/shard_map/pallas_call | solution.py:308
  28.9 1.5 %copy.14 = f32[2,16,512]{2,1,0:T(8,128)} copy(f32[2,16,512]{2,1,0:T(8,128)} %get-tuple-element.4) | data formatting | bytes 131072
  30.4 1.5 %copy.15 = f32[2,16,512]{2,1,0:T(8,128)} copy(f32[2,16,512]{2,1,0:T(8,128)} %get-tuple-element.5) | data formatting | bytes 131072

commit v2 on v1

--- a/solution.py
+++ b/solution.py
@@ -10,7 +10,7 @@
 MESH = pl.DeviceIdType.MESH
 F32 = jnp.float32
 BF16 = jnp.bfloat16
-TILE = 8
+TILE = 16
 HALF = TILE // 2
 
 
@@ -23,11 +23,10 @@
 
 
 def times_i(x):
-    rows, cols = x.shape
-    x = x.reshape(rows // TILE, TILE, cols)
-    turned = pltpu.roll(x, HALF, 1)
-    upper = lax.broadcasted_iota(jnp.int32, x.shape, 1) < HALF
-    return jnp.where(upper, -turned, turned).reshape(rows, cols)
+    parts = []
+    for lo in range(0, x.shape[0], TILE):
+        parts += [-x[lo + HALF : lo + TILE], x[lo : lo + HALF]]
+    return jnp.concatenate(parts, axis=0)
 
 
 def kernel(
@@ -42,8 +41,10 @@
     group_coupling,
     outer_expand,
     ranks,
-    first,
-    second,
+    first_near,
+    first_far,
+    second_near,
+    second_far,
     v_in,
     nb,
     ib,
@@ -59,6 +60,7 @@
     cbuf,
     fbuf,
     kmat,
+    emat,
     acc,
     load_sem,
     nbr_send,
@@ -75,9 +77,8 @@
     rank_cap = ib.shape[1]
     group_rank = ob.shape[1]
     pages = wide_send.shape[1]
-    stride = n_blk // pages
-    slot = pos // stride
-    reducer = lax.rem(pos, stride) == 0
+    places = [n_blk // 2 - pages + 2 * k for k in range(pages)]
+    reducer = functools.reduce(jnp.logical_or, [pos == place for place in places])
 
     loads = [
         pltpu.make_async_copy(probes, v_in, load_sem.at[0]),
@@ -113,7 +114,6 @@
     start = jnp.concatenate(
         [parts[c][k * HALF : (k + 1) * HALF] for k in range(pages) for c in range(2)], axis=0
     )
-    pl.semaphore_wait(barrier, n_blk - 1 + (n_reg - 1) * pages)
 
     def to_next(a):
         return pltpu.make_async_remote_copy(
@@ -142,18 +142,23 @@
         vec, ivec = full.astype(BF16), times_i(full).astype(BF16)
         vbuf[a] = vec
 
-        @pl.when(pos < n_blk - 1)
-        def _():
-            to_next(a).start()
-
-        @pl.when(pos > 0)
-        def _():
-            to_prev(a).start()
+        def send_vec():
+            @pl.when(pos < n_blk - 1)
+            def _():
+                to_next(a).start()
+
+            @pl.when(pos > 0)
+            def _():
+                to_prev(a).start()
 
         if a == 0:
             loads[1].wait()
+        else:
+            send_vec()
         wide = dot_t(vec, ob[0]) + dot_t(ivec, ob[1])
-        wide_send[a] = wide.reshape(pages, TILE, group_rank)
+        wide_send[a] = wide.astype(BF16).reshape(pages, TILE, group_rank)
+        if a == 0:
+            pl.semaphore_wait(barrier, n_blk - 1 + (n_reg - 1) * pages)
         for off in range(1, n_reg):
             for k in range(pages):
                 pltpu.make_async_remote_copy(
@@ -161,16 +166,20 @@
                     dst_ref=wide_recv.at[a, off - 1, pos],
                     send_sem=wide_ssem.at[a],
                     recv_sem=wide_rsem.at[a],
-                    device_id=(lax.rem(region + off, n_reg), k * stride),
+                    device_id=(lax.rem(region + off, n_reg), places[k]),
                     device_id_type=MESH,
                 ).start()
 
         if a == 0:
+            send_vec()
             loads[2].wait()
         coeff = dot_t(vec, ib[0]) + dot_t(ivec, ib[1])
         keep = lax.broadcasted_iota(jnp.int32, coeff.shape, 1) < ranks[0]
         coeff = jnp.where(keep, coeff, 0.0)
-        cbuf[a, pos] = jnp.concatenate([coeff, times_i(coeff)], axis=1).astype(BF16)
+        groups = range(0, pages * TILE, TILE)
+        real = jnp.concatenate([coeff[lo : lo + HALF] for lo in groups], axis=0)
+        imag = jnp.concatenate([coeff[lo + HALF : lo + TILE] for lo in groups], axis=0)
+        cbuf[a, pos] = jnp.concatenate([real, imag], axis=1).astype(BF16)
         for off in range(1, n_blk):
             pltpu.make_async_remote_copy(
                 src_ref=cbuf.at[a, pos],
@@ -186,17 +195,6 @@
         acc[...] = dot_t(vec, nb[1, 0]) + dot_t(ivec, nb[1, 1])
 
         if a == 0:
-            loads[4].wait()
-            width = 2 * rank_cap
-            lower = lax.broadcasted_iota(jnp.int32, (rank_cap, width), 1) < rank_cap
-            for t in range(n_blk // 2):
-                re = cp[0, :, t * width : (t + 1) * width].astype(F32)
-                im = cp[1, :, t * width : (t + 1) * width].astype(F32)
-                even = jnp.where(lower, re, pltpu.roll(im, rank_cap, 1))
-                odd = jnp.where(lower, pltpu.roll(re, rank_cap, 1), im)
-                for j, block in ((2 * t, even), (2 * t + 1, odd)):
-                    far = (jnp.abs(pos - j) > 1).astype(F32)
-                    kmat[:, j * width : (j + 1) * width] = (block * far).astype(BF16)
             loads[5].wait()
 
         @pl.when(reducer)
@@ -204,25 +202,30 @@
             wait_bytes(wide_recv.at[a], wide_rsem.at[a])
             field = jnp.zeros((2 * TILE, group_rank), F32)
             for off in range(1, n_reg):
-                total = wide_recv[a, off - 1, 0]
+                total = wide_recv[a, off - 1, 0].astype(F32)
                 for j in range(1, n_blk):
-                    total = total + wide_recv[a, off - 1, j]
+                    total = total + wide_recv[a, off - 1, j].astype(F32)
                 high = total.astype(BF16).astype(F32)
                 both = jnp.concatenate([high, total - high], axis=0)
                 source = lax.rem(region - off + n_reg, n_reg)
                 columns = pl.ds(pl.multiple_of(source * group_rank, group_rank), group_rank)
                 field = field + dot_t(both.astype(BF16), gc[0, :, columns])
                 field = field + dot_t(times_i(both).astype(BF16), gc[1, :, columns])
-            fbuf[a, slot] = (field[:TILE] + field[TILE:]).astype(BF16).astype(F32)
-            for off in range(1, n_blk):
-                pltpu.make_async_remote_copy(
-                    src_ref=fbuf.at[a, slot],
-                    dst_ref=fbuf.at[a, slot],
-                    send_sem=f_ssem.at[a],
-                    recv_sem=f_rsem.at[a],
-                    device_id=(region, lax.rem(pos + off, n_blk)),
-                    device_id_type=MESH,
-                ).start()
+            page = (field[:TILE] + field[TILE:]).astype(BF16)
+            for k, place in enumerate(places):
+
+                @pl.when(pos == place)
+                def _():
+                    fbuf[a, k] = page
+                    for off in range(1, n_blk):
+                        pltpu.make_async_remote_copy(
+                            src_ref=fbuf.at[a, k],
+                            dst_ref=fbuf.at[a, k],
+                            send_sem=f_ssem.at[a],
+                            recv_sem=f_rsem.at[a],
+                            device_id=(region, (place + off) % n_blk),
+                            device_id_type=MESH,
+                        ).start()
 
         if a == 0:
             loads[6].wait()
@@ -242,12 +245,43 @@
             turned = times_i(after.astype(F32)).astype(BF16)
             acc[...] += dot_t(after, nb[2, 0]) + dot_t(turned, nb[2, 1])
 
+        if a == 0:
+            loads[4].wait()
+            pair = 2 * rank_cap
+            lower = lax.broadcasted_iota(jnp.int32, (rank_cap, pair), 1) < rank_cap
+            for t in range(n_blk // 2):
+                re = cp[0, :, t * pair : (t + 1) * pair].astype(F32)
+                im = cp[1, :, t * pair : (t + 1) * pair].astype(F32)
+                re_turned = pltpu.roll(re, rank_cap, 1)
+                im_turned = pltpu.roll(im, rank_cap, 1)
+                for j, top, low in (
+                    (2 * t, (re, -im_turned), (im, re_turned)),
+                    (2 * t + 1, (re_turned, -im), (im_turned, re)),
+                ):
+                    far = (jnp.abs(pos - j) > 1).astype(F32)
+                    at = slice(j * pair, (j + 1) * pair)
+                    kmat[:rank_cap, at] = (jnp.where(lower, *top) * far).astype(BF16)
+                    kmat[rank_cap:, at] = (jnp.where(lower, *low) * far).astype(BF16)
+            loads[8].wait()
+            width = ie.shape[2]
+            emat[:rank_cap, :width] = ie[0]
+            emat[rank_cap:, :width] = (-ie[1].astype(F32)).astype(BF16)
+            emat[:rank_cap, width:] = ie[1]
+            emat[rank_cap:, width:] = ie[0]
+
         wait_bytes(cbuf.at[a, pl.ds(0, n_blk - 1)], c_rsem.at[a])
         piece = jnp.concatenate([cbuf[a, j] for j in range(n_blk)], axis=1)
-        inner = dot_t(piece, kmat[...])
-        if a == 0:
-            loads[8].wait()
-        acc[...] += dot(inner.astype(BF16), ie[0]) + dot(times_i(inner).astype(BF16), ie[1])
+        inner = dot_t(piece, kmat[...]).astype(BF16)
+        spread = dot(inner, emat[...])
+        half = spread.shape[1] // 2
+        acc[...] += jnp.concatenate(
+            [
+                spread[k * HALF : (k + 1) * HALF, c * half : (c + 1) * half]
+                for k in range(pages)
+                for c in range(2)
+            ],
+            axis=0,
+        )
 
         if a == 0:
             loads[9].wait()
@@ -261,7 +295,8 @@
             wait_bytes(fbuf.at[a], f_rsem.at[a])
 
         field = fbuf[a].reshape(pages * TILE, group_rank)
-        return acc[...] + dot(field.astype(BF16), oe[0]) + dot(times_i(field).astype(BF16), oe[1])
+        turned = times_i(field.astype(F32)).astype(BF16)
+        return acc[...], dot(field, oe[0]) + dot(turned, oe[1])
 
     def put(out, full):
         for k in range(pages):
@@ -269,10 +304,12 @@
                 lo = k * TILE + c * HALF
                 out[c, k * HALF : (k + 1) * HALF, :] = full[lo : lo + HALF]
 
-    one = apply(0, start)
-    put(first, one)
-    two = apply(1, one)
-    put(second, two)
+    near, far = apply(0, start)
+    put(first_near, near)
+    put(first_far, far)
+    near, far = apply(1, near + far)
+    put(second_near, near)
+    put(second_far, far)
 
     for a in range(2):
 
@@ -305,12 +342,12 @@
         rank_cap, group_rank = inner_basis.shape[1], outer_basis.shape[1]
         out = jax.ShapeDtypeStruct(probes.shape, F32)
         dma = pltpu.SemaphoreType.DMA
-        return pl.pallas_call(
+        parts = pl.pallas_call(
             functools.partial(kernel, n_reg, n_blk),
-            out_shape=(out, out),
+            out_shape=(out,) * 4,
             in_specs=[pl.BlockSpec(memory_space=pl.ANY)] * 8
             + [pl.BlockSpec(memory_space=pltpu.SMEM)],
-            out_specs=(pl.BlockSpec(memory_space=pltpu.VMEM),) * 2,
+            out_specs=(pl.BlockSpec(memory_space=pltpu.VMEM),) * 4,
             scratch_shapes=[
                 pltpu.VMEM(x.shape, BF16)
                 for x in (
@@ -327,11 +364,12 @@
             + [
                 pltpu.VMEM((2, rows, width), BF16),
                 pltpu.VMEM((2, 2, rows, width), BF16),
-                pltpu.VMEM((2, pages, TILE, group_rank), F32),
-                pltpu.VMEM((2, n_reg - 1, n_blk, TILE, group_rank), F32),
-                pltpu.VMEM((2, n_blk, rows, 2 * rank_cap), BF16),
-                pltpu.VMEM((2, pages, TILE, group_rank), F32),
-                pltpu.VMEM((rank_cap, n_blk * 2 * rank_cap), BF16),
+                pltpu.VMEM((2, pages, TILE, group_rank), BF16),
+                pltpu.VMEM((2, n_reg - 1, n_blk, TILE, group_rank), BF16),
+                pltpu.VMEM((2, n_blk, vectors, 2 * rank_cap), BF16),
+                pltpu.VMEM((2, pages, TILE, group_rank), BF16),
+                pltpu.VMEM((2 * rank_cap, n_blk * 2 * rank_cap), BF16),
+                pltpu.VMEM((2 * rank_cap, 2 * width), BF16),
                 pltpu.VMEM((rows, width), F32),
                 dma((10,)),
                 dma((2, 2)),
@@ -347,6 +385,7 @@
                 collective_id=0, has_side_effects=True, vmem_limit_bytes=56 * 2**20
             ),
         )(*args)
+        return parts[0] + parts[1], parts[2] + parts[3]
 
     placed = (
         P(None, None, both),

time: 32.4 us -> 28.3 us (0.87)
  Pallas kernels: 27.6 us -> 23.5 us
  other arithmetic: 0 us -> 3.02 us
  local copies, waits for them, and re-layouts: 2.95 us -> 0 us
    pallas_call x1, Pallas kernels: 27.6 us -> 23.5 us  [local(): pl.pallas_call(functools.partial(kernel, n_reg, n_blk), out_shape=(out,)...]
    add x0 -> x2, other arithmetic: none -> 3.02 us  [local(): return (parts[0] + parts[1], parts[2] + parts[3])]
    unnamed x2 -> x0, local copies, waits for them, and re-layouts: 2.95 us -> none
where the time goes in v2:
time: 28.3 us; the launch traced here: 27.8 us
  Pallas kernels  23.5 us (83%)
  other arithmetic  3.02 us (11%)
  between operations  1.29 us (5%)
    pallas_call x1, Pallas kernels, local(): pl.pallas_call(functools.partial(kernel, n_reg, n_blk), out_shape=(out,)...  23.5 us
    add x2, other arithmetic, local(): return (parts[0] + parts[1], parts[2] + parts[3])  3.02 us

profile of v2, /device:TPU:1, one launch (start us, length us, event | category | flops | bytes accessed | tf_op | source)
XLA Modules:
  0.0 27.8 jit_solution(1200347912533782686)
XLA Ops:
  1.3 23.5 %shard_map.104 = (f32[2,16,512]{2,1,0:T(8,128)}, f32[2,16,512]{2,1,0:T(8,128)}, f32[2,16,512]{2,1,0:T(8,128)}, f32[2,16,512]{2,1,0:T(8,128)}) custom-call(bf16[2,16,512]{2,1,0:T(8,128)(2,1)} %probes.1, bf16[3,2,512,512]{3,2,1,0:T(8,128)(2,1)} %near_blocks.1, bf16[2,64,512]{2,1,0:T(8,128)(2,1)} %inner_basis.1, bf16[2,64,512]{2,1,0:T(8,128)(2,1)} %coupling.1, ...), custom_call_target="tpu_custom_call" | custom-call | tf_op jit(solution)/shard_map/pallas_call | solution.py:345
  24.8 1.5 %add.6 = f32[2,16,512]{2,1,0:T(8,128)} add(f32[2,16,512]{2,1,0:T(8,128)} %get-tuple-element.6, f32[2,16,512]{2,1,0:T(8,128)} %get-tuple-element.7) | non-fusion elementwise | flops 16384 | bytes 196608 | tf_op jit(solution)/shard_map/add | solution.py:388
  26.3 1.5 %add.7 = f32[2,16,512]{2,1,0:T(8,128)} add(f32[2,16,512]{2,1,0:T(8,128)} %get-tuple-element.8, f32[2,16,512]{2,1,0:T(8,128)} %get-tuple-element.9) | non-fusion elementwise | flops 16384 | bytes 196608 | tf_op jit(solution)/shard_map/add | solution.py:388

commit v3 on v2

--- a/solution.py
+++ b/solution.py
@@ -41,10 +41,8 @@
     group_coupling,
     outer_expand,
     ranks,
-    first_near,
-    first_far,
-    second_near,
-    second_far,
+    first,
+    second,
     v_in,
     nb,
     ib,
@@ -92,8 +90,8 @@
         pltpu.make_async_copy(inner_expand, ie, load_sem.at[8]),
         pltpu.make_async_copy(outer_expand, oe, load_sem.at[9]),
     ]
-    for load in loads:
-        load.start()
+    loads[0].start()
+    loads[1].start()
 
     barrier = pltpu.get_barrier_semaphore()
     for off in range(1, n_blk):
@@ -109,6 +107,8 @@
                     barrier, inc=1, device_id=(lax.rem(region + off, n_reg), j), device_id_type=MESH
                 )
 
+    for load in loads[2:]:
+        load.start()
     loads[0].wait()
     parts = [v_in[0].astype(F32), v_in[1].astype(F32)]
     start = jnp.concatenate(
@@ -153,8 +153,6 @@
 
         if a == 0:
             loads[1].wait()
-        else:
-            send_vec()
         wide = dot_t(vec, ob[0]) + dot_t(ivec, ob[1])
         wide_send[a] = wide.astype(BF16).reshape(pages, TILE, group_rank)
         if a == 0:
@@ -165,13 +163,13 @@
                     src_ref=wide_send.at[a, k],
                     dst_ref=wide_recv.at[a, off - 1, pos],
                     send_sem=wide_ssem.at[a],
-                    recv_sem=wide_rsem.at[a],
+                    recv_sem=wide_rsem.at[a, off - 1],
                     device_id=(lax.rem(region + off, n_reg), places[k]),
                     device_id_type=MESH,
                 ).start()
 
-        if a == 0:
-            send_vec()
+        send_vec()
+        if a == 0:
             loads[2].wait()
         coeff = dot_t(vec, ib[0]) + dot_t(ivec, ib[1])
         keep = lax.broadcasted_iota(jnp.int32, coeff.shape, 1) < ranks[0]
@@ -199,9 +197,9 @@
 
         @pl.when(reducer)
         def _():
-            wait_bytes(wide_recv.at[a], wide_rsem.at[a])
             field = jnp.zeros((2 * TILE, group_rank), F32)
             for off in range(1, n_reg):
+                wait_bytes(wide_recv.at[a, off - 1], wide_rsem.at[a, off - 1])
                 total = wide_recv[a, off - 1, 0].astype(F32)
                 for j in range(1, n_blk):
                     total = total + wide_recv[a, off - 1, j].astype(F32)
@@ -296,7 +294,7 @@
 
         field = fbuf[a].reshape(pages * TILE, group_rank)
         turned = times_i(field.astype(F32)).astype(BF16)
-        return acc[...], dot(field, oe[0]) + dot(turned, oe[1])
+        return acc[...] + (dot(field, oe[0]) + dot(turned, oe[1]))
 
     def put(out, full):
         for k in range(pages):
@@ -304,12 +302,9 @@
                 lo = k * TILE + c * HALF
                 out[c, k * HALF : (k + 1) * HALF, :] = full[lo : lo + HALF]
 
-    near, far = apply(0, start)
-    put(first_near, near)
-    put(first_far, far)
-    near, far = apply(1, near + far)
-    put(second_near, near)
-    put(second_far, far)
+    one = apply(0, start)
+    put(first, one)
+    put(second, apply(1, one))
 
     for a in range(2):
 
@@ -327,6 +322,17 @@
         @pl.when(reducer)
         def _():
             wait_bytes(wide_recv.at[a, 0, pl.ds(0, n_blk - 1)], f_ssem.at[a])
+
+
+def store(first, second, first_out, second_out, sem):
+    copies = [
+        pltpu.make_async_copy(first, first_out, sem.at[0]),
+        pltpu.make_async_copy(second, second_out, sem.at[1]),
+    ]
+    for copy in copies:
+        copy.start()
+    for copy in copies:
+        copy.wait()
 
 
 def solution(mesh):
@@ -340,14 +346,14 @@
         rows = 2 * vectors
         pages = rows // TILE
         rank_cap, group_rank = inner_basis.shape[1], outer_basis.shape[1]
-        out = jax.ShapeDtypeStruct(probes.shape, F32)
+        out = pltpu.VMEM(probes.shape, F32)
         dma = pltpu.SemaphoreType.DMA
         parts = pl.pallas_call(
             functools.partial(kernel, n_reg, n_blk),
-            out_shape=(out,) * 4,
+            out_shape=(out,) * 2,
             in_specs=[pl.BlockSpec(memory_space=pl.ANY)] * 8
             + [pl.BlockSpec(memory_space=pltpu.SMEM)],
-            out_specs=(pl.BlockSpec(memory_space=pltpu.VMEM),) * 4,
+            out_specs=(pl.BlockSpec(memory_space=pltpu.VMEM),) * 2,
             scratch_shapes=[
                 pltpu.VMEM(x.shape, BF16)
                 for x in (
@@ -375,7 +381,7 @@
                 dma((2, 2)),
                 dma((2, 2)),
                 dma((2,)),
-                dma((2,)),
+                dma((2, n_reg - 1)),
                 dma((2,)),
                 dma((2,)),
                 dma((2,)),
@@ -385,7 +391,14 @@
                 collective_id=0, has_side_effects=True, vmem_limit_bytes=56 * 2**20
             ),
         )(*args)
-        return parts[0] + parts[1], parts[2] + parts[3]
+        result = jax.ShapeDtypeStruct(probes.shape, F32)
+        return pl.pallas_call(
+            store,
+            out_shape=(result, result),
+            in_specs=[pl.BlockSpec(memory_space=pltpu.VMEM)] * 2,
+            out_specs=(pl.BlockSpec(memory_space=pl.ANY),) * 2,
+            scratch_shapes=[dma((2,))],
+        )(*parts)
 
     placed = (
         P(None, None, both),

time: 28.3 us -> 27.4 us (0.968)
  other arithmetic: 3.02 us -> 0 us
  local copies, waits for them, and re-layouts: 0 us -> 1.23 us
  Pallas kernels: 23.5 us -> 24.4 us
    add x2 -> x0, other arithmetic: 3.02 us -> none  [local(): return (parts[0] + parts[1], parts[2] + parts[3])]
    pallas_call x0 -> x1, Pallas kernels: none -> 1.54 us  [local(): pl.pallas_call(store, out_shape=(result, result), in_specs=[pl.BlockSpec(...]
    unnamed x0 -> x4, local copies, waits for them, and re-layouts: none -> 1.23 us
    pallas_call x1, Pallas kernels: 23.5 us -> 22.9 us  [local(): pl.pallas_call(functools.partial(kernel, n_reg, n_blk), out_shape=(out,)...]
where the time goes in v3:
time: 27.4 us; the launch traced here: 26.9 us
  Pallas kernels  24.4 us (89%)
  between operations  1.3 us (5%)
  local copies, waits for them, and re-layouts  1.23 us (4%)
    pallas_call x1, Pallas kernels, local(): pl.pallas_call(functools.partial(kernel, n_reg, n_blk), out_shape=(out,)...  22.9 us
    pallas_call x1, Pallas kernels, local(): pl.pallas_call(store, out_shape=(result, result), in_specs=[pl.BlockSpec(...  1.54 us
    unnamed x4, local copies, waits for them, and re-layouts  1.23 us

profile of v3, /device:TPU:1, one launch (start us, length us, event | category | flops | bytes accessed | tf_op | source)
XLA Modules:
  0.0 26.9 jit_solution(1278660883772266376)
XLA Ops:
  1.3 22.9 %shard_map.104 = (f32[2,16,512]{2,1,0:T(8,128)S(1)}, f32[2,16,512]{2,1,0:T(8,128)S(1)}) custom-call(bf16[2,16,512]{2,1,0:T(8,128)(2,1)} %probes.1, bf16[3,2,512,512]{3,2,1,0:T(8,128)(2,1)} %near_blocks.1, bf16[2,64,512]{2,1,0:T(8,128)(2,1)} %inner_basis.1, bf16[2,64,512]{2,1,0:T(8,128)(2,1)} %coupling.1, bf16[2,64,512]{2,1,0:T(8,128)(2,1)} %inner_expand.1, ...), custom_call_target="tpu_custom_call" | custom-call | tf_op jit(solution)/shard_map/pallas_call | solution.py:351
  24.1 0.0 copy-start
  24.2 0.6 %copy-done = f32[2,16,512]{2,1,0:T(8,128)} copy-done((f32[2,16,512]{2,1,0:T(8,128)}, f32[2,16,512]{2,1,0:T(8,128)S(1)}, u32[]{:S(2)}) %copy-start) | copy-done | bytes 65560
  24.8 0.0 copy-start.1
  24.8 0.6 %copy-done.1 = f32[2,16,512]{2,1,0:T(8,128)} copy-done((f32[2,16,512]{2,1,0:T(8,128)}, f32[2,16,512]{2,1,0:T(8,128)S(1)}, u32[]{:S(2)}) %copy-start.1) | copy-done | bytes 65560
  25.4 1.5 %shard_map.105 = (f32[2,16,512]{2,1,0:T(8,128)}, f32[2,16,512]{2,1,0:T(8,128)}) custom-call(f32[2,16,512]{2,1,0:T(8,128)} %copy-done, f32[2,16,512]{2,1,0:T(8,128)} %copy-done.1), custom_call_target="tpu_custom_call" | custom-call | tf_op jit(solution)/shard_map/pallas_call | solution.py:395
Async XLA Ops:
  24.1 0.6 %copy-start = (f32[2,16,512]{2,1,0:T(8,128)}, f32[2,16,512]{2,1,0:T(8,128)S(1)}, u32[]{:S(2)}) copy-start(f32[2,16,512]{2,1,0:T(8,128)S(1)} %get-tuple-element.4.first) | copy-start | bytes 196612
  24.8 0.6 %copy-start.1 = (f32[2,16,512]{2,1,0:T(8,128)}, f32[2,16,512]{2,1,0:T(8,128)S(1)}, u32[]{:S(2)}) copy-start(f32[2,16,512]{2,1,0:T(8,128)S(1)} %get-tuple-element.5.second) | copy-start | bytes 196612

commit v4 on v3

--- a/solution.py
+++ b/solution.py
@@ -193,6 +193,16 @@
         acc[...] = dot_t(vec, nb[1, 0]) + dot_t(ivec, nb[1, 1])
 
         if a == 0:
+            loads[6].wait()
+
+        @pl.when(pos > 0)
+        def _():
+            wait_bytes(nbr.at[a, 0], nbr_recv.at[a, 0])
+            before = nbr[a, 0]
+            turned = times_i(before.astype(F32)).astype(BF16)
+            acc[...] += dot_t(before, nb[0, 0]) + dot_t(turned, nb[0, 1])
+
+        if a == 0:
             loads[5].wait()
 
         @pl.when(reducer)
@@ -226,15 +236,7 @@
                         ).start()
 
         if a == 0:
-            loads[6].wait()
             loads[7].wait()
-
-        @pl.when(pos > 0)
-        def _():
-            wait_bytes(nbr.at[a, 0], nbr_recv.at[a, 0])
-            before = nbr[a, 0]
-            turned = times_i(before.astype(F32)).astype(BF16)
-            acc[...] += dot_t(before, nb[0, 0]) + dot_t(turned, nb[0, 1])
 
         @pl.when(pos < n_blk - 1)
         def _():
@@ -324,17 +326,6 @@
             wait_bytes(wide_recv.at[a, 0, pl.ds(0, n_blk - 1)], f_ssem.at[a])
 
 
-def store(first, second, first_out, second_out, sem):
-    copies = [
-        pltpu.make_async_copy(first, first_out, sem.at[0]),
-        pltpu.make_async_copy(second, second_out, sem.at[1]),
-    ]
-    for copy in copies:
-        copy.start()
-    for copy in copies:
-        copy.wait()
-
-
 def solution(mesh):
     n_reg, n_blk = mesh.shape["region"], mesh.shape["blk"]
     both = ("region", "blk")
@@ -348,7 +339,7 @@
         rank_cap, group_rank = inner_basis.shape[1], outer_basis.shape[1]
         out = pltpu.VMEM(probes.shape, F32)
         dma = pltpu.SemaphoreType.DMA
-        parts = pl.pallas_call(
+        return pl.pallas_call(
             functools.partial(kernel, n_reg, n_blk),
             out_shape=(out,) * 2,
             in_specs=[pl.BlockSpec(memory_space=pl.ANY)] * 8
@@ -391,14 +382,6 @@
                 collective_id=0, has_side_effects=True, vmem_limit_bytes=56 * 2**20
             ),
         )(*args)
-        result = jax.ShapeDtypeStruct(probes.shape, F32)
-        return pl.pallas_call(
-            store,
-            out_shape=(result, result),
-            in_specs=[pl.BlockSpec(memory_space=pltpu.VMEM)] * 2,
-            out_specs=(pl.BlockSpec(memory_space=pl.ANY),) * 2,
-            scratch_shapes=[dma((2,))],
-        )(*parts)
 
     placed = (
         P(None, None, both),

time: 27.4 us -> 25.9 us (0.945)
  Pallas kernels: 24.4 us -> 22.9 us
    pallas_call x1 -> x0, Pallas kernels: 1.54 us -> none  [local(): pl.pallas_call(store, out_shape=(result, result), in_specs=[pl.BlockSpec(...]
    unnamed x4 -> x2, local copies, waits for them, and re-layouts: 1.23 us -> 1.26 us
where the time goes in v4:
time: 25.9 us; the launch traced here: 25.4 us
  Pallas kernels  22.9 us (88%)
  between operations  1.29 us (5%)
  local copies, waits for them, and re-layouts  1.26 us (5%)
    pallas_call x1, Pallas kernels, local(): pl.pallas_call(functools.partial(kernel, n_reg, n_blk), out_shape=(out,)...  22.9 us
    unnamed x2, local copies, waits for them, and re-layouts  1.26 us

profile of v4, /device:TPU:1, one launch (start us, length us, event | category | flops | bytes accessed | tf_op | source)
XLA Modules:
  0.0 25.4 jit_solution(17672658658618890363)
XLA Ops:
  1.3 22.9 %shard_map.104 = (f32[2,16,512]{2,1,0:T(8,128)S(1)}, f32[2,16,512]{2,1,0:T(8,128)S(1)}) custom-call(bf16[2,16,512]{2,1,0:T(8,128)(2,1)} %probes.1, bf16[3,2,512,512]{3,2,1,0:T(8,128)(2,1)} %near_blocks.1, bf16[2,64,512]{2,1,0:T(8,128)(2,1)} %inner_basis.1, bf16[2,64,512]{2,1,0:T(8,128)(2,1)} %coupling.1, bf16[2,64,512]{2,1,0:T(8,128)(2,1)} %inner_expand.1, ...), custom_call_target="tpu_custom_call" | custom-call | tf_op jit(solution)/shard_map/pallas_call | solution.py:342
  24.1 0.6 %copy.13 = f32[2,16,512]{2,1,0:T(8,128)} copy(f32[2,16,512]{2,1,0:T(8,128)S(1)} %get-tuple-element.2) | data formatting | bytes 131072
  24.8 0.6 %copy.14 = f32[2,16,512]{2,1,0:T(8,128)} copy(f32[2,16,512]{2,1,0:T(8,128)S(1)} %get-tuple-element.3) | data formatting | bytes 131072

commit v5 on v4

--- a/solution.py
+++ b/solution.py
@@ -55,6 +55,8 @@
     nbr,
     wide_send,
     wide_recv,
+    sum_send,
+    sum_recv,
     cbuf,
     fbuf,
     kmat,
@@ -65,6 +67,8 @@
     nbr_recv,
     wide_ssem,
     wide_rsem,
+    s_ssem,
+    s_rsem,
     c_ssem,
     c_rsem,
     f_ssem,
@@ -102,10 +106,9 @@
     @pl.when(reducer)
     def _():
         for off in range(1, n_reg):
-            for j in range(n_blk):
-                pl.semaphore_signal(
-                    barrier, inc=1, device_id=(lax.rem(region + off, n_reg), j), device_id_type=MESH
-                )
+            pl.semaphore_signal(
+                barrier, inc=1, device_id=(lax.rem(region + off, n_reg), pos), device_id_type=MESH
+            )
 
     for load in loads[2:]:
         load.start()
@@ -154,19 +157,34 @@
         if a == 0:
             loads[1].wait()
         wide = dot_t(vec, ob[0]) + dot_t(ivec, ob[1])
-        wide_send[a] = wide.astype(BF16).reshape(pages, TILE, group_rank)
-        if a == 0:
-            pl.semaphore_wait(barrier, n_blk - 1 + (n_reg - 1) * pages)
-        for off in range(1, n_reg):
-            for k in range(pages):
+        wide = wide.astype(BF16).reshape(pages, TILE, group_rank)
+        wide_send[a] = wide
+        if a == 0:
+
+            @pl.when(reducer)
+            def _():
+                pl.semaphore_wait(barrier, n_blk - 1 + n_reg - 1)
+
+            @pl.when(jnp.logical_not(reducer))
+            def _():
+                pl.semaphore_wait(barrier, n_blk - 1)
+
+        for k, place in enumerate(places):
+
+            @pl.when(pos != place)
+            def _():
                 pltpu.make_async_remote_copy(
                     src_ref=wide_send.at[a, k],
-                    dst_ref=wide_recv.at[a, off - 1, pos],
+                    dst_ref=wide_recv.at[a, pos],
                     send_sem=wide_ssem.at[a],
-                    recv_sem=wide_rsem.at[a, off - 1],
-                    device_id=(lax.rem(region + off, n_reg), places[k]),
+                    recv_sem=wide_rsem.at[a],
+                    device_id=(region, place),
                     device_id_type=MESH,
                 ).start()
+
+            @pl.when(pos == place)
+            def _():
+                wide_recv[a, place] = wide[k]
 
         send_vec()
         if a == 0:
@@ -188,6 +206,23 @@
                 device_id_type=MESH,
             ).start()
 
+        @pl.when(reducer)
+        def _():
+            wait_bytes(wide_recv.at[a, pl.ds(0, n_blk - 1)], wide_rsem.at[a])
+            total = wide_recv[a, 0].astype(F32)
+            for j in range(1, n_blk):
+                total = total + wide_recv[a, j].astype(F32)
+            sum_send[a] = total
+            for off in range(1, n_reg):
+                pltpu.make_async_remote_copy(
+                    src_ref=sum_send.at[a],
+                    dst_ref=sum_recv.at[a, off - 1],
+                    send_sem=s_ssem.at[a],
+                    recv_sem=s_rsem.at[a, off - 1],
+                    device_id=(lax.rem(region + off, n_reg), pos),
+                    device_id_type=MESH,
+                ).start()
+
         if a == 0:
             loads[3].wait()
         acc[...] = dot_t(vec, nb[1, 0]) + dot_t(ivec, nb[1, 1])
@@ -209,10 +244,8 @@
         def _():
             field = jnp.zeros((2 * TILE, group_rank), F32)
             for off in range(1, n_reg):
-                wait_bytes(wide_recv.at[a, off - 1], wide_rsem.at[a, off - 1])
-                total = wide_recv[a, off - 1, 0].astype(F32)
-                for j in range(1, n_blk):
-                    total = total + wide_recv[a, off - 1, j].astype(F32)
+                wait_bytes(sum_recv.at[a, off - 1], s_rsem.at[a, off - 1])
+                total = sum_recv[a, off - 1]
                 high = total.astype(BF16).astype(F32)
                 both = jnp.concatenate([high, total - high], axis=0)
                 source = lax.rem(region - off + n_reg, n_reg)
@@ -318,12 +351,17 @@
         def _():
             to_prev(a).wait_send()
 
-        wait_bytes(wide_recv.at[a, :, pl.ds(0, pages)], wide_ssem.at[a])
         wait_bytes(cbuf.at[a, pl.ds(0, n_blk - 1)], c_ssem.at[a])
 
         @pl.when(reducer)
         def _():
-            wait_bytes(wide_recv.at[a, 0, pl.ds(0, n_blk - 1)], f_ssem.at[a])
+            wait_bytes(wide_send.at[a, pl.ds(0, pages - 1)], wide_ssem.at[a])
+            wait_bytes(sum_recv.at[a], s_ssem.at[a])
+            wait_bytes(wide_recv.at[a, pl.ds(0, n_blk - 1)], f_ssem.at[a])
+
+        @pl.when(jnp.logical_not(reducer))
+        def _():
+            wait_bytes(wide_send.at[a], wide_ssem.at[a])
 
 
 def solution(mesh):
@@ -362,7 +400,9 @@
                 pltpu.VMEM((2, rows, width), BF16),
                 pltpu.VMEM((2, 2, rows, width), BF16),
                 pltpu.VMEM((2, pages, TILE, group_rank), BF16),
-                pltpu.VMEM((2, n_reg - 1, n_blk, TILE, group_rank), BF16),
+                pltpu.VMEM((2, n_blk, TILE, group_rank), BF16),
+                pltpu.VMEM((2, TILE, group_rank), F32),
+                pltpu.VMEM((2, n_reg - 1, TILE, group_rank), F32),
                 pltpu.VMEM((2, n_blk, vectors, 2 * rank_cap), BF16),
                 pltpu.VMEM((2, pages, TILE, group_rank), BF16),
                 pltpu.VMEM((2 * rank_cap, n_blk * 2 * rank_cap), BF16),
@@ -371,6 +411,8 @@
                 dma((10,)),
                 dma((2, 2)),
                 dma((2, 2)),
+                dma((2,)),
+                dma((2,)),
                 dma((2,)),
                 dma((2, n_reg - 1)),
                 dma((2,)),

time: 25.9 us -> 29.4 us (1.14)
  Pallas kernels: 22.9 us -> 26.3 us
    pallas_call x1, Pallas kernels: 22.9 us -> 26.3 us  [local(): pl.pallas_call(functools.partial(kernel, n_reg, n_blk), out_shape=(out,)...]
where the time goes in v5:
time: 29.4 us; the launch traced here: 28.9 us
  Pallas kernels  26.3 us (89%)
  between operations  1.29 us (4%)
  local copies, waits for them, and re-layouts  1.26 us (4%)
    pallas_call x1, Pallas kernels, local(): pl.pallas_call(functools.partial(kernel, n_reg, n_blk), out_shape=(out,)...  26.3 us
    unnamed x2, local copies, waits for them, and re-layouts  1.26 us

profile of v5, /device:TPU:1, one launch (start us, length us, event | category | flops | bytes accessed | tf_op | source)
XLA Modules:
  0.0 28.9 jit_solution(3634658630325977610)
XLA Ops:
  1.3 26.3 %shard_map.104 = (f32[2,16,512]{2,1,0:T(8,128)S(1)}, f32[2,16,512]{2,1,0:T(8,128)S(1)}) custom-call(bf16[2,16,512]{2,1,0:T(8,128)(2,1)} %probes.1, bf16[3,2,512,512]{3,2,1,0:T(8,128)(2,1)} %near_blocks.1, bf16[2,64,512]{2,1,0:T(8,128)(2,1)} %inner_basis.1, bf16[2,64,512]{2,1,0:T(8,128)(2,1)} %coupling.1, bf16[2,64,512]{2,1,0:T(8,128)(2,1)} %inner_expand.1, ...), custom_call_target="tpu_custom_call" | custom-call | tf_op jit(solution)/shard_map/pallas_call | solution.py:380
  27.6 0.6 %copy.13 = f32[2,16,512]{2,1,0:T(8,128)} copy(f32[2,16,512]{2,1,0:T(8,128)S(1)} %get-tuple-element.2) | data formatting | bytes 131072
  28.3 0.6 %copy.14 = f32[2,16,512]{2,1,0:T(8,128)} copy(f32[2,16,512]{2,1,0:T(8,128)S(1)} %get-tuple-element.3) | data formatting | bytes 131072
